TPU v7x, 256 devices: a whole 4x4x8 slice. The times are simulated.
256 devices in a mesh: span: 32 (over z_hi, x, core), head: 8 (over z_lo, y).
Axes of the slice: x: 4, y: 4, z: 8 (z_hi: 4, z_lo: 2; z = z_hi * 2 + z_lo), core: 2. Of those that a mesh axis runs over, the one named last changes fastest.
Arguments:
- queries: bfloat16 [8192, 6144], P(('span', 'head')), may hold values from -35 to 35
- keys: bfloat16 [8192, 1024], P(('span', 'head')), may hold values from -4 to 4
- values: bfloat16 [8192, 1024], P(('span', 'head')), may hold values from -6 to 6
- tile_mask: int32 [4, 16, 64], replicated, may hold values from 0 to 1, as said below
- noise_level: int32 [4], replicated, may hold values from 0 to 15
- level_gate: float32 [16, 6144], replicated, may hold values from 0.25 to 1.75
Outputs:
- gated_attention: bfloat16 [8192, 6144], P(('span', 'head'))
Inputs may be any that keep to these rules, and one draw needn't show every extreme that they name: tile_mask[c, b, c * 16 + b] = 1 for every group c and query tile b; entries for key tiles of groups after c are 0.
All inputs are finite; a program needn't handle non-finite values.
Results may differ from a plain program's by a relative error of at most 0.009.
Values may be sent and summed in bfloat16 or wider, within the bound.
A program may use at most 64 MiB of HBM per device.

v0:
```python
import jax
import jax.numpy as jnp
from jax import lax
from jax.sharding import PartitionSpec as P

HEADS = 48
KV_HEADS = 8
HEAD_DIM = 128
GROUPS = 4
TILE = 128


def slice_mask(tile_mask, group_number, first_block, block_count):
    window = lax.dynamic_slice(
        tile_mask, (group_number, first_block, jnp.int32(0)), (1, block_count, tile_mask.shape[2])
    )
    return window[0]


def empty_state(kv_groups, per_group, row_count):
    return (
        jnp.full((kv_groups, per_group, row_count), -1e30, jnp.float32),
        jnp.zeros((kv_groups, per_group, row_count), jnp.float32),
        jnp.zeros((kv_groups, per_group, row_count, HEAD_DIM), jnp.float32),
    )


def attend_block(state, query_four, row_mask, key_block, value_block, key_first):
    block_rows = key_block.shape[0]
    columns = lax.dynamic_slice_in_dim(row_mask, key_first // TILE, block_rows // TILE, 1)

    def compute(current):
        running_max, running_sum, summed = current
        allowed = jnp.repeat(jnp.repeat(columns > 0, TILE, axis=0), TILE, axis=1)
        scores = jnp.einsum(
            "rkgd,pkd->kgrp", query_four, key_block, preferred_element_type=jnp.float32
        )
        scores = jnp.where(allowed, scores * HEAD_DIM ** (-0.5), -1e30)
        new_max = jnp.maximum(running_max, jnp.max(scores, axis=-1))
        weights = jnp.where(allowed, jnp.exp(scores - new_max[..., None]), 0.0)
        factor = jnp.exp(running_max - new_max)
        running_sum = running_sum * factor + jnp.sum(weights, axis=-1)
        summed = summed * factor[..., None] + jnp.einsum(
            "kgrp,pkd->kgrd",
            weights.astype(jnp.bfloat16),
            value_block,
            preferred_element_type=jnp.float32,
        )
        return (new_max, running_sum, summed)

    return lax.cond(jnp.any(columns > 0), compute, lambda current: current, state)


def finish(state):
    running_max, running_sum, summed = state
    result = summed / running_sum[..., None]
    kv_groups, per_group, row_count, depth = result.shape
    result = jnp.transpose(result, (2, 0, 1, 3)).reshape(row_count, kv_groups * per_group * depth)
    return result.astype(jnp.bfloat16)


def body(queries, keys, values, tile_mask, noise_level, level_gate):
    q_rows, k_rows, v_rows = (
        lax.all_to_all(queries, "head", split_axis=1, concat_axis=0, tiled=True),
        lax.all_to_all(keys, "head", split_axis=1, concat_axis=0, tiled=True),
        lax.all_to_all(values, "head", split_axis=1, concat_axis=0, tiled=True),
    )
    row_count = q_rows.shape[0]
    kv_groups = k_rows.shape[1] // HEAD_DIM
    per_group = HEADS // KV_HEADS
    split_count = lax.axis_size("span") // GROUPS
    position = lax.axis_index("span")
    own_group = position // split_count
    segment = position % split_count
    own_blocks = row_count // TILE
    query_four = q_rows.reshape(row_count, kv_groups, per_group, HEAD_DIM)
    query_sets = ((query_four, slice_mask(tile_mask, own_group, segment * own_blocks, own_blocks)),)
    start_states = tuple(
        (empty_state(kv_groups, per_group, entry[0].shape[0]) for entry in query_sets)
    )
    key_piece = lax.all_gather(k_rows, "span", axis=0, tiled=True)
    value_piece = lax.all_gather(v_rows, "span", axis=0, tiled=True)
    length = key_piece.shape[0]
    shards = length // row_count
    per_step = max(1, 512 // row_count)
    while shards % per_step:
        per_step = per_step - 1
    block_rows = row_count * per_step
    key_four = key_piece.reshape(length // block_rows, block_rows, kv_groups, HEAD_DIM)
    value_four = value_piece.reshape(length // block_rows, block_rows, kv_groups, HEAD_DIM)

    def advance(block_index, current):
        key_block = lax.dynamic_index_in_dim(key_four, block_index, 0, keepdims=False)
        value_block = lax.dynamic_index_in_dim(value_four, block_index, 0, keepdims=False)
        key_first = block_index * block_rows
        return tuple(
            (
                attend_block(state, entry[0], entry[1], key_block, value_block, key_first)
                for state, entry in zip(current, query_sets)
            )
        )

    states = lax.fori_loop(0, length // block_rows, advance, start_states)
    attended = finish(states[0])
    token_rows = lax.all_to_all(attended, "head", split_axis=0, concat_axis=1, tiled=True)
    level_index = jnp.sum(jnp.where(jnp.arange(GROUPS) == own_group, noise_level, 0))
    selector = (jnp.arange(level_gate.shape[0]) == level_index).astype(jnp.float32)
    gate_row = jnp.dot(selector[None, :], level_gate, precision=lax.Precision.HIGHEST)[0]
    return (token_rows.astype(jnp.float32) * gate_row[None, :]).astype(jnp.bfloat16)


def solution(mesh):
    return jax.shard_map(
        body,
        mesh=mesh,
        in_specs=(
            P(("span", "head"), None),
            P(("span", "head"), None),
            P(("span", "head"), None),
            P(),
            P(),
            P(),
        ),
        out_specs=P(("span", "head"), None),
        check_vma=False,
    )
```

profile of v0, /device:TPU:192, one launch (start us, length us, event | category | flops | bytes accessed | tf_op | source)
XLA Modules:
  0.0 242.3 jit_solution(2317654709322780407)
XLA Ops:
  6.5 0.9 copy_bitcast_fusion.2
  7.4 11.2 %all_to_all.64 = bf16[32,8,128]{2,0,1:T(8,128)(2,1)} all-to-all(bf16[32,8,128]{2,0,1:T(8,128)(2,1)S(1)} %copy_bitcast_fusion.2), channel_id=1, replica_groups=mesh['span'=32,'head'=8] {'head'}, dimensions={1} | all-to-all | bytes 131072 | tf_op jit(solution)/shard_map/all_to_all | solution.py:65
  18.7 0.9 copy_bitcast_fusion.1
  19.6 9.4 %all_to_all.65 = bf16[32,8,128]{2,0,1:T(8,128)(2,1)} all-to-all(bf16[32,8,128]{2,0,1:T(8,128)(2,1)S(1)} %copy_bitcast_fusion.1), channel_id=1, replica_groups=mesh['span'=32,'head'=8] {'head'}, dimensions={1} | all-to-all | bytes 131072 | tf_op jit(solution)/shard_map/all_to_all | solution.py:66
  29.0 1.8 copy.44
  30.8 3.5 %all-to-all-start.1 = ((bf16[32,8,768]{2,0,1:T(8,128)(2,1)}), bf16[32,8,768]{2,0,1:T(8,128)(2,1)S(1)}, u32[]{:S(2)}, u32[]{:S(2)}) async-start(bf16[32,8,768]{2,0,1:T(8,128)(2,1)} %bitcast.96), calls=%async_computation.1 | async-start | bytes 786432 | tf_op jit(solution)/shard_map/all_to_all | solution.py:64
  34.9 7.0 %all-to-all-done.1 = bf16[32,8,768]{2,0,1:T(8,128)(2,1)S(1)} async-done(((bf16[32,8,768]{2,0,1:T(8,128)(2,1)}), bf16[32,8,768]{2,0,1:T(8,128)(2,1)S(1)}, u32[]{:S(2)}, u32[]{:S(2)}) %all-to-all-start.1) | async-done | bytes 393248 | tf_op jit(solution)/shard_map/all_to_all | solution.py:64
  42.5 26.6 %all-gather.3.cloned.1.call-done = bf16[8192,128]{1,0:T(8,128)(2,1)} async-done(((bf16[256,128]{1,0:T(8,128)(2,1)}), bf16[8192,128]{1,0:T(8,128)(2,1)}) %all-gather.3.cloned.1.call-update) | async-done | bytes 2097168 | tf_op jit(solution)/shard_map/all_gather | solution.py:81
  69.1 54.3 %all-gather.5.cloned.1.call-done = bf16[8192,128]{1,0:T(8,128)(2,1)} async-done(((bf16[256,128]{1,0:T(8,128)(2,1)}), bf16[8192,128]{1,0:T(8,128)(2,1)}) %all-gather.5.cloned.1.call-update) | async-done | bytes 2097168 | tf_op jit(solution)/shard_map/all_gather | solution.py:82
  123.5 97.1 %while.19 = (s32[]{:T(128)}, f32[1,6,256]{2,1,0:T(8,128)S(1)}, f32[1,6,256]{2,1,0:T(8,128)S(1)}, f32[1,6,256,128]{3,2,1,0:T(8,128)S(1)}, s32[2,64]{1,0:T(2,128)S...) while((s32[]{:T(128)}, f32[1,6,256]{2,1,0:T(8,128)S(1)}, ...), condition=%wide.region_6.7_spmd, body=%wide.region_0.6_spmd.sunk | while | flops 413274656 | bytes 12290669 | solution.py:103
  124.9 4.7 %conditional.2 = ((f32[1,6,256]{2,1,0:T(8,128)S(1)}, f32[1,6,256]{2,1,0:T(8,128)S(1)}, f32[1,6,256,128]{3,2,1,0:T(8,128)S(1)})) conditional(s32[]{:T(128)} %convert_element_type.62, (f32[1,6,256]{2,1,0:T(8,128)S(1)}, f32[1,6,256]{2,1,0:T(8,128)S(1)}, f32[1,6,256,128]{3,2,1,0:T(8,128)S(1)}) %tuple.64, (s32[2,4]{1,0:T(2,128)S(1)}, s32[]{:T(128)}, ...), branch_computations={%region_2.2_spmd, %region_3.5_spmd} | conditional | flops 413274624 | bytes 12290170 | solution.py:51
  125.0 1.5 fusion
  126.6 2.1 fusion.10
  128.7 0.8 fusion.2
  130.9 4.7 %conditional.2 = ((f32[1,6,256]{2,1,0:T(8,128)S(1)}, f32[1,6,256]{2,1,0:T(8,128)S(1)}, f32[1,6,256,128]{3,2,1,0:T(8,128)S(1)})) conditional(s32[]{:T(128)} %convert_element_type.62, (f32[1,6,256]{2,1,0:T(8,128)S(1)}, f32[1,6,256]{2,1,0:T(8,128)S(1)}, f32[1,6,256,128]{3,2,1,0:T(8,128)S(1)}) %tuple.64, (s32[2,4]{1,0:T(2,128)S(1)}, s32[]{:T(128)}, ...), branch_computations={%region_2.2_spmd, %region_3.5_spmd} | conditional | flops 413274624 | bytes 12290170 | solution.py:51
  131.1 1.5 fusion
  132.6 2.1 fusion.10
  137.0 4.7 %conditional.2 = ((f32[1,6,256]{2,1,0:T(8,128)S(1)}, f32[1,6,256]{2,1,0:T(8,128)S(1)}, f32[1,6,256,128]{3,2,1,0:T(8,128)S(1)})) conditional(s32[]{:T(128)} %convert_element_type.62, (f32[1,6,256]{2,1,0:T(8,128)S(1)}, f32[1,6,256]{2,1,0:T(8,128)S(1)}, f32[1,6,256,128]{3,2,1,0:T(8,128)S(1)}) %tuple.64, (s32[2,4]{1,0:T(2,128)S(1)}, s32[]{:T(128)}, ...), branch_computations={%region_2.2_spmd, %region_3.5_spmd} | conditional | flops 413274624 | bytes 12290170 | solution.py:51
  137.2 1.5 fusion
  138.7 2.1 fusion.10
  143.1 4.7 %conditional.2 = ((f32[1,6,256]{2,1,0:T(8,128)S(1)}, f32[1,6,256]{2,1,0:T(8,128)S(1)}, f32[1,6,256,128]{3,2,1,0:T(8,128)S(1)})) conditional(s32[]{:T(128)} %convert_element_type.62, (f32[1,6,256]{2,1,0:T(8,128)S(1)}, f32[1,6,256]{2,1,0:T(8,128)S(1)}, f32[1,6,256,128]{3,2,1,0:T(8,128)S(1)}) %tuple.64, (s32[2,4]{1,0:T(2,128)S(1)}, s32[]{:T(128)}, ...), branch_computations={%region_2.2_spmd, %region_3.5_spmd} | conditional | flops 413274624 | bytes 12290170 | solution.py:51
  143.2 1.5 fusion
  144.8 2.1 fusion.10
  149.1 4.7 %conditional.2 = ((f32[1,6,256]{2,1,0:T(8,128)S(1)}, f32[1,6,256]{2,1,0:T(8,128)S(1)}, f32[1,6,256,128]{3,2,1,0:T(8,128)S(1)})) conditional(s32[]{:T(128)} %convert_element_type.62, (f32[1,6,256]{2,1,0:T(8,128)S(1)}, f32[1,6,256]{2,1,0:T(8,128)S(1)}, f32[1,6,256,128]{3,2,1,0:T(8,128)S(1)}) %tuple.64, (s32[2,4]{1,0:T(2,128)S(1)}, s32[]{:T(128)}, ...), branch_computations={%region_2.2_spmd, %region_3.5_spmd} | conditional | flops 413274624 | bytes 12290170 | solution.py:51
  149.3 1.5 fusion
  150.9 2.1 fusion.10
  155.2 4.7 %conditional.2 = ((f32[1,6,256]{2,1,0:T(8,128)S(1)}, f32[1,6,256]{2,1,0:T(8,128)S(1)}, f32[1,6,256,128]{3,2,1,0:T(8,128)S(1)})) conditional(s32[]{:T(128)} %convert_element_type.62, (f32[1,6,256]{2,1,0:T(8,128)S(1)}, f32[1,6,256]{2,1,0:T(8,128)S(1)}, f32[1,6,256,128]{3,2,1,0:T(8,128)S(1)}) %tuple.64, (s32[2,4]{1,0:T(2,128)S(1)}, s32[]{:T(128)}, ...), branch_computations={%region_2.2_spmd, %region_3.5_spmd} | conditional | flops 413274624 | bytes 12290170 | solution.py:51
  155.4 1.5 fusion
  156.9 2.1 fusion.10
  161.3 4.7 %conditional.2 = ((f32[1,6,256]{2,1,0:T(8,128)S(1)}, f32[1,6,256]{2,1,0:T(8,128)S(1)}, f32[1,6,256,128]{3,2,1,0:T(8,128)S(1)})) conditional(s32[]{:T(128)} %convert_element_type.62, (f32[1,6,256]{2,1,0:T(8,128)S(1)}, f32[1,6,256]{2,1,0:T(8,128)S(1)}, f32[1,6,256,128]{3,2,1,0:T(8,128)S(1)}) %tuple.64, (s32[2,4]{1,0:T(2,128)S(1)}, s32[]{:T(128)}, ...), branch_computations={%region_2.2_spmd, %region_3.5_spmd} | conditional | flops 413274624 | bytes 12290170 | solution.py:51
  161.4 1.5 fusion
  163.0 2.1 fusion.10
  167.4 4.7 %conditional.2 = ((f32[1,6,256]{2,1,0:T(8,128)S(1)}, f32[1,6,256]{2,1,0:T(8,128)S(1)}, f32[1,6,256,128]{3,2,1,0:T(8,128)S(1)})) conditional(s32[]{:T(128)} %convert_element_type.62, (f32[1,6,256]{2,1,0:T(8,128)S(1)}, f32[1,6,256]{2,1,0:T(8,128)S(1)}, f32[1,6,256,128]{3,2,1,0:T(8,128)S(1)}) %tuple.64, (s32[2,4]{1,0:T(2,128)S(1)}, s32[]{:T(128)}, ...), branch_computations={%region_2.2_spmd, %region_3.5_spmd} | conditional | flops 413274624 | bytes 12290170 | solution.py:51
  167.5 1.5 fusion
  169.1 2.1 fusion.10
  173.4 4.7 %conditional.2 = ((f32[1,6,256]{2,1,0:T(8,128)S(1)}, f32[1,6,256]{2,1,0:T(8,128)S(1)}, f32[1,6,256,128]{3,2,1,0:T(8,128)S(1)})) conditional(s32[]{:T(128)} %convert_element_type.62, (f32[1,6,256]{2,1,0:T(8,128)S(1)}, f32[1,6,256]{2,1,0:T(8,128)S(1)}, f32[1,6,256,128]{3,2,1,0:T(8,128)S(1)}) %tuple.64, (s32[2,4]{1,0:T(2,128)S(1)}, s32[]{:T(128)}, ...), branch_computations={%region_2.2_spmd, %region_3.5_spmd} | conditional | flops 413274624 | bytes 12290170 | solution.py:51
  173.6 1.5 fusion
  175.1 2.1 fusion.10
  179.5 4.7 %conditional.2 = ((f32[1,6,256]{2,1,0:T(8,128)S(1)}, f32[1,6,256]{2,1,0:T(8,128)S(1)}, f32[1,6,256,128]{3,2,1,0:T(8,128)S(1)})) conditional(s32[]{:T(128)} %convert_element_type.62, (f32[1,6,256]{2,1,0:T(8,128)S(1)}, f32[1,6,256]{2,1,0:T(8,128)S(1)}, f32[1,6,256,128]{3,2,1,0:T(8,128)S(1)}) %tuple.64, (s32[2,4]{1,0:T(2,128)S(1)}, s32[]{:T(128)}, ...), branch_computations={%region_2.2_spmd, %region_3.5_spmd} | conditional | flops 413274624 | bytes 12290170 | solution.py:51
  179.7 1.5 fusion
  181.2 2.1 fusion.10
  185.6 4.7 %conditional.2 = ((f32[1,6,256]{2,1,0:T(8,128)S(1)}, f32[1,6,256]{2,1,0:T(8,128)S(1)}, f32[1,6,256,128]{3,2,1,0:T(8,128)S(1)})) conditional(s32[]{:T(128)} %convert_element_type.62, (f32[1,6,256]{2,1,0:T(8,128)S(1)}, f32[1,6,256]{2,1,0:T(8,128)S(1)}, f32[1,6,256,128]{3,2,1,0:T(8,128)S(1)}) %tuple.64, (s32[2,4]{1,0:T(2,128)S(1)}, s32[]{:T(128)}, ...), branch_computations={%region_2.2_spmd, %region_3.5_spmd} | conditional | flops 413274624 | bytes 12290170 | solution.py:51
  185.7 1.5 fusion
  187.3 2.1 fusion.10
  191.6 4.7 %conditional.2 = ((f32[1,6,256]{2,1,0:T(8,128)S(1)}, f32[1,6,256]{2,1,0:T(8,128)S(1)}, f32[1,6,256,128]{3,2,1,0:T(8,128)S(1)})) conditional(s32[]{:T(128)} %convert_element_type.62, (f32[1,6,256]{2,1,0:T(8,128)S(1)}, f32[1,6,256]{2,1,0:T(8,128)S(1)}, f32[1,6,256,128]{3,2,1,0:T(8,128)S(1)}) %tuple.64, (s32[2,4]{1,0:T(2,128)S(1)}, s32[]{:T(128)}, ...), branch_computations={%region_2.2_spmd, %region_3.5_spmd} | conditional | flops 413274624 | bytes 12290170 | solution.py:51
  191.8 1.5 fusion
  193.4 2.1 fusion.10
  197.7 4.7 %conditional.2 = ((f32[1,6,256]{2,1,0:T(8,128)S(1)}, f32[1,6,256]{2,1,0:T(8,128)S(1)}, f32[1,6,256,128]{3,2,1,0:T(8,128)S(1)})) conditional(s32[]{:T(128)} %convert_element_type.62, (f32[1,6,256]{2,1,0:T(8,128)S(1)}, f32[1,6,256]{2,1,0:T(8,128)S(1)}, f32[1,6,256,128]{3,2,1,0:T(8,128)S(1)}) %tuple.64, (s32[2,4]{1,0:T(2,128)S(1)}, s32[]{:T(128)}, ...), branch_computations={%region_2.2_spmd, %region_3.5_spmd} | conditional | flops 413274624 | bytes 12290170 | solution.py:51
  197.9 1.5 fusion
  199.4 2.1 fusion.10
  203.8 4.7 %conditional.2 = ((f32[1,6,256]{2,1,0:T(8,128)S(1)}, f32[1,6,256]{2,1,0:T(8,128)S(1)}, f32[1,6,256,128]{3,2,1,0:T(8,128)S(1)})) conditional(s32[]{:T(128)} %convert_element_type.62, (f32[1,6,256]{2,1,0:T(8,128)S(1)}, f32[1,6,256]{2,1,0:T(8,128)S(1)}, f32[1,6,256,128]{3,2,1,0:T(8,128)S(1)}) %tuple.64, (s32[2,4]{1,0:T(2,128)S(1)}, s32[]{:T(128)}, ...), branch_computations={%region_2.2_spmd, %region_3.5_spmd} | conditional | flops 413274624 | bytes 12290170 | solution.py:51
  203.9 1.5 fusion
  205.5 2.1 fusion.10
  209.9 4.7 %conditional.2 = ((f32[1,6,256]{2,1,0:T(8,128)S(1)}, f32[1,6,256]{2,1,0:T(8,128)S(1)}, f32[1,6,256,128]{3,2,1,0:T(8,128)S(1)})) conditional(s32[]{:T(128)} %convert_element_type.62, (f32[1,6,256]{2,1,0:T(8,128)S(1)}, f32[1,6,256]{2,1,0:T(8,128)S(1)}, f32[1,6,256,128]{3,2,1,0:T(8,128)S(1)}) %tuple.64, (s32[2,4]{1,0:T(2,128)S(1)}, s32[]{:T(128)}, ...), branch_computations={%region_2.2_spmd, %region_3.5_spmd} | conditional | flops 413274624 | bytes 12290170 | solution.py:51
  210.0 1.5 fusion
  211.6 2.1 fusion.10
  215.9 4.7 %conditional.2 = ((f32[1,6,256]{2,1,0:T(8,128)S(1)}, f32[1,6,256]{2,1,0:T(8,128)S(1)}, f32[1,6,256,128]{3,2,1,0:T(8,128)S(1)})) conditional(s32[]{:T(128)} %convert_element_type.62, (f32[1,6,256]{2,1,0:T(8,128)S(1)}, f32[1,6,256]{2,1,0:T(8,128)S(1)}, f32[1,6,256,128]{3,2,1,0:T(8,128)S(1)}) %tuple.64, (s32[2,4]{1,0:T(2,128)S(1)}, s32[]{:T(128)}, ...), branch_computations={%region_2.2_spmd, %region_3.5_spmd} | conditional | flops 413274624 | bytes 12290170 | solution.py:51
  216.1 1.5 fusion
  217.6 2.1 fusion.10
  221.2 1.2 convert_element_type.41
  222.4 4.4 %all-to-all-start.3 = ((bf16[8,32,768]{2,1,0:T(8,128)(2,1)}), bf16[8,32,768]{2,1,0:T(8,128)(2,1)S(1)}, u32[]{:S(2)}, u32[]{:S(2)}) async-start(bf16[8,32,768]{2,1,0:T(8,128)(2,1)} %convert_element_type.41), calls=%async_computation.3 | async-start | bytes 786432 | tf_op jit(solution)/shard_map/all_to_all | solution.py:105
  227.4 0.8 fusion.26
  228.2 6.3 %all-to-all-done.3 = bf16[8,32,768]{2,1,0:T(8,128)(2,1)S(1)} async-done(((bf16[8,32,768]{2,1,0:T(8,128)(2,1)}), bf16[8,32,768]{2,1,0:T(8,128)(2,1)S(1)}, u32[]{:S(2)}, u32[]{:S(2)}) %all-to-all-start.3) | async-done | bytes 393248 | tf_op jit(solution)/shard_map/all_to_all | solution.py:105
  234.6 0.8 multiply_convert_fusion
  (146 shorter events, 27.6 us)
Async XLA Ops:
  6.5 220.9 %copy-start = (f32[16,6144]{1,0:T(8,128)S(1)}, f32[16,6144]{1,0:T(8,128)}, u32[]{:S(2)}) copy-start(f32[16,6144]{1,0:T(8,128)} %param.15) | copy-start | bytes 1179652
  6.5 62.6 %all-gather.3.cloned.1.call-start = ((), (), s32[]{:S(2)}) async-start(), calls=%async_computation.4 | async-start | bytes 2162688 | tf_op jit(solution)/shard_map/all_gather | solution.py:81
  18.6 104.7 %all-gather.5.cloned.1.call-start = ((), (), s32[]{:S(2)}) async-start(), calls=%async_computation.5 | async-start | bytes 2162688 | tf_op jit(solution)/shard_map/all_gather | solution.py:82
  30.8 11.2 %all-to-all-start.1 = ((bf16[32,8,768]{2,0,1:T(8,128)(2,1)}), bf16[32,8,768]{2,0,1:T(8,128)(2,1)S(1)}, u32[]{:S(2)}, u32[]{:S(2)}) async-start(bf16[32,8,768]{2,0,1:T(8,128)(2,1)} %bitcast.96), calls=%async_computation.1 | async-start | bytes 786432 | tf_op jit(solution)/shard_map/all_to_all | solution.py:64
  220.6 6.2 %copy-start.1 = (s32[4]{0:T(128)S(1)}, s32[4]{0:T(128)}, u32[]{:S(2)}) copy-start(s32[4]{0:T(128)} %param.14) | copy-start | bytes 52
  222.4 12.1 %all-to-all-start.3 = ((bf16[8,32,768]{2,1,0:T(8,128)(2,1)}), bf16[8,32,768]{2,1,0:T(8,128)(2,1)S(1)}, u32[]{:S(2)}, u32[]{:S(2)}) async-start(bf16[8,32,768]{2,1,0:T(8,128)(2,1)} %convert_element_type.41), calls=%async_computation.3 | async-start | bytes 786432 | tf_op jit(solution)/shard_map/all_to_all | solution.py:105
Sparse Core Ops, SparseCore 0:
  18.8 50.2 all-gather.2
  71.7 51.6 all-gather.4
where the time goes:
time: 245 us; the launch traced here: 242 us
  waiting for transfers between devices  94.3 us (38%)
  matrix products  59.7 us (24%)
  other arithmetic  25.6 us (10%)
  blocking collectives  20.6 us (8%)
  between operations  13.5 us (6%)
  loops' own time  12.4 us (5%)
  local copies, waits for them, and re-layouts  8.24 us (3%)
  starting transfers between devices  7.86 us (3%)
    all_gather x1, waiting for transfers between devices, body(): value_piece = lax.all_gather(v_rows, 'span', axis=0, tiled=True)  54.3 us
    dot_general x16, matrix products, compute(): jnp.einsum('kgrp,pkd->kgrd', weights.astype(jnp.bfloat16), value_block, p...  34.3 us
    all_gather x1, waiting for transfers between devices, body(): key_piece = lax.all_gather(k_rows, 'span', axis=0, tiled=True)  26.6 us
    dot_general x16, matrix products, compute(): jnp.einsum('rkgd,pkd->kgrp', query_four, key_block, preferred_element_typ...  24.6 us
    reduce_sum x16, other arithmetic, compute(): running_sum = running_sum * factor + jnp.sum(weights, axis=-1)  12.2 us
    reduce_or x16, other arithmetic, attend_block(): jnp.any(columns > 0)  11.3 us
    another operation x1, loops' own time, body(): states = lax.fori_loop(0, length // block_rows, advance, start_states)  11.2 us
    all_to_all x1, blocking collectives, body(): lax.all_to_all(keys, 'head', split_axis=1, concat_axis=0, tiled=True)  11.2 us
  transfers between devices with their start and end apart: 4, of which 4 were waited for; matrix products, arithmetic and copies ran while one was open for 2% of the time, Pallas kernels for 0%

commit v1 on v0

v1 whole, which is shorter than its diff:
```python
import functools
import math

import jax
import jax.numpy as jnp
from jax import lax
from jax.experimental import pallas as pl
from jax.experimental.pallas import tpu as pltpu
from jax.sharding import PartitionSpec as P

HEADS = 48
KV_HEADS = 8
HEAD_DIM = 128
GROUPS = 4
TILE = 128
PER_KV = HEADS // KV_HEADS
PER_CORE = PER_KV // 2
ROWS = 32
QCOLS = PER_CORE * HEAD_DIM
SCALE = math.log2(math.e) / math.sqrt(HEAD_DIM)
BLOCKED = -1e30
MESH = pl.DeviceIdType.MESH
NX, NY, NZ, NC = 4, 4, 8, 2


def device(x, y, z, core):
    return (((z // 2) * NX + x) * NC + core, (z % 2) * NY + y)


def attend_step(kc, kx, first, kbuf, vbuf, qbuf, qbias, top, total):
    keys = kbuf[kc, kx].reshape(NZ * TILE, HEAD_DIM)
    values = vbuf[kc, kx].reshape(NZ * TILE, HEAD_DIM)
    lane = lax.broadcasted_iota(jnp.int32, (TILE, HEAD_DIM), 1)
    marks = []
    for kz in range(NZ):
        tile = ((kz // 2) * NX + kx) * 4 + kc * 2 + kz % 2
        marks.append((lane == tile).astype(jnp.float32).astype(jnp.bfloat16))
    keys = jnp.concatenate([keys, jnp.concatenate(marks, axis=0)], axis=1)
    values = jnp.concatenate([values, jnp.ones_like(values)], axis=1)
    for g in range(GROUPS):
        count = (g + 1) * 2 * TILE
        rows = qbuf[2 * g : 2 * g + 2].reshape(TILE, QCOLS)
        bias = qbias[g]
        query = jnp.concatenate(
            [
                jnp.concatenate([rows[:, j * HEAD_DIM : (j + 1) * HEAD_DIM], bias], axis=1)
                for j in range(PER_CORE)
            ],
            axis=0,
        )
        scores = lax.dot_general(
            query, keys[:count], (((1,), (1,)), ((), ())), preferred_element_type=jnp.float32
        )
        old = top[g]
        new = jnp.maximum(old, jnp.max(scores, axis=1, keepdims=True))
        factor = jnp.exp2((old - new) * SCALE)
        wide = jnp.concatenate([new] * (count // HEAD_DIM), axis=1)
        weights = jnp.exp2((scores - wide) * SCALE).astype(jnp.bfloat16)
        part = lax.dot_general(
            weights, values[:count], (((1,), (0,)), ((), ())), preferred_element_type=jnp.float32
        )
        total[g] = total[g] * jnp.concatenate([factor, factor], axis=1) + part
        top[g] = new


def kernel(
    q_hbm,
    k_hbm,
    v_hbm,
    mask_ref,
    out_ref,
    kbuf,
    vbuf,
    qbuf,
    obuf,
    qbias,
    top,
    total,
    kz_send,
    kz_recv,
    vz_send,
    vz_recv,
    q_send,
    q_recv,
    kx_send,
    kx_recv,
    ky_send,
    ky_recv,
    vy_send,
    vy_recv,
    vx_send,
    vx_recv,
    sib_send,
    sib_recv,
    o_send,
    o_recv,
):
    span, head = lax.axis_index("span"), lax.axis_index("head")
    core = span % NC
    x = (span // NC) % NX
    z = (span // (NC * NX)) * 2 + head // NY
    y = head % NY

    def back(at, step, size):
        return (at + size - step) % size

    def ahead(at, step, size):
        return (at + step) % size

    def send(src, dst, send_sem, recv_sem, target):
        return pltpu.make_async_remote_copy(
            src_ref=src,
            dst_ref=dst,
            send_sem=send_sem,
            recv_sem=recv_sem,
            device_id=target,
            device_id_type=MESH,
        )

    barrier = pltpu.get_barrier_semaphore()
    peers = [device(x, y, ahead(z, d, NZ), c) for d in range(1, NZ) for c in range(NC)]
    peers.append(device(x, y, z, 1 - core))
    peers += [device(ahead(x, d, NX), y, z, core) for d in range(1, NX)]
    peers += [device(x, ahead(y, d, NY), z, core) for d in range(1, NY)]
    for peer in peers:
        pl.semaphore_signal(barrier, inc=1, device_id=peer, device_id_type=MESH)
    pl.semaphore_wait(barrier, len(peers))

    def columns(at, width):
        return pl.ds(pl.multiple_of(at * width, width), width)

    order = (4, 3, 5, 2, 6, 1, 7)
    sends = []
    for hbm, buf, send_sems, recv_sems in (
        (k_hbm, kbuf, kz_send, kz_recv),
        (v_hbm, vbuf, vz_send, vz_recv),
    ):
        for d in order:
            to = ahead(z, d, NZ)
            sends.append(
                send(
                    hbm.at[:, columns(to, HEAD_DIM)],
                    buf.at[core, x, z, y],
                    send_sems.at[d],
                    recv_sems.at[d],
                    device(x, y, to, core),
                )
            )
            sends[-1].start()
        pltpu.make_async_copy(
            hbm.at[:, columns(z, HEAD_DIM)], buf.at[core, x, z, y], recv_sems.at[0]
        ).start()
    for d in order + (0,):
        for e in range(NC):
            to = ahead(z, d, NZ)
            to_core = (core + e) % NC
            source = q_hbm.at[:, columns(to * NC + to_core, QCOLS)]
            if d == 0 and e == 0:
                pltpu.make_async_copy(source, qbuf.at[z, core], q_recv.at[0, 0]).start()
                continue
            sends.append(
                send(
                    source,
                    qbuf.at[z, core],
                    q_send.at[d, e],
                    q_recv.at[d, e],
                    device(x, y, to, to_core),
                )
            )
            sends[-1].start()

    for g in range(GROUPS):
        for low in range(2):
            for c in range(NC):
                row = mask_ref[g, pl.ds((x * NC + c) * 2 + low, 1), :]
                row = jnp.where(row > 0, 0.0, BLOCKED)
                row = jnp.concatenate([row, jnp.zeros_like(row)], axis=1)
                at = (low * NC + c) * ROWS
                qbias[g, at : at + ROWS, :] = jnp.broadcast_to(row, (ROWS, HEAD_DIM)).astype(
                    jnp.bfloat16
                )
    top[...] = jnp.full_like(top, BLOCKED)
    total[...] = jnp.zeros_like(total)

    def wait_in(buf_at, sem):
        pltpu.make_async_copy(buf_at, buf_at, sem).wait()

    for d in range(NZ):
        wait_in(kbuf.at[core, x, back(z, d, NZ), y], kz_recv.at[d])

    def send_keys(dx):
        chunk = kbuf.at[core, back(x, dx, NX), :, y]
        for dy in range(1, NY):
            sends.append(
                send(
                    chunk,
                    chunk,
                    ky_send.at[dx, dy],
                    ky_recv.at[dx, dy],
                    device(x, ahead(y, dy, NY), z, core),
                )
            )
            sends[-1].start()

    def send_values(dy):
        chunk = vbuf.at[core, x, :, back(y, dy, NY)]
        for dx in range(1, NX):
            sends.append(
                send(
                    chunk,
                    chunk,
                    vx_send.at[dx, dy],
                    vx_recv.at[dx, dy],
                    device(ahead(x, dx, NX), y, z, core),
                )
            )
            sends[-1].start()

    own_keys = kbuf.at[core, x, :, y]
    for dx in (2, 1, 3):
        sends.append(
            send(own_keys, own_keys, kx_send.at[dx], kx_recv.at[dx], device(ahead(x, dx, NX), y, z, core))
        )
        sends[-1].start()
    for d in range(NZ):
        wait_in(vbuf.at[core, x, back(z, d, NZ), y], vz_recv.at[d])
    own_values = vbuf.at[core, x, :, y]
    for dy in (2, 1, 3):
        sends.append(
            send(own_values, own_values, vy_send.at[dy], vy_recv.at[dy], device(x, ahead(y, dy, NY), z, core))
        )
        sends[-1].start()
    send_keys(0)
    send_values(0)
    for d in (1, 3, 2):
        wait_in(kbuf.at[core, back(x, d, NX), :, y], kx_recv.at[d])
        send_keys(d)
        wait_in(vbuf.at[core, x, :, back(y, d, NY)], vy_recv.at[d])
        send_values(d)

    for d in range(NZ):
        for e in range(NC):
            wait_in(qbuf.at[back(z, d, NZ), (core + e) % NC], q_recv.at[d, e])

    def to_sibling(buf, at, which):
        chunk = buf.at[core, at]
        return send(
            chunk, chunk, sib_send.at[which], sib_recv.at[which], device(x, y, z, 1 - core)
        )

    def advance(i, carry):
        dx = i // 2
        far = i % 2
        at = (x + NX - dx) % NX

        @pl.when(far == 0)
        def _():
            for dy in range(1, NY):
                wait_in(kbuf.at[core, at, :, back(y, dy, NY)], ky_recv.at[dx, dy])

            @pl.when(dx > 0)
            def _():
                for dy in range(NY):
                    wait_in(vbuf.at[core, at, :, back(y, dy, NY)], vx_recv.at[dx, dy])

            to_sibling(kbuf, at, dx * 2).start()
            to_sibling(vbuf, at, dx * 2 + 1).start()

        @pl.when(far == 1)
        def _():
            wait_in(kbuf.at[1 - core, at], sib_recv.at[dx * 2])
            wait_in(vbuf.at[1 - core, at], sib_recv.at[dx * 2 + 1])

        attend_step((core + far) % NC, at, i == 0, kbuf, vbuf, qbuf, qbias, top, total)
        return carry

    lax.fori_loop(0, 2 * NX, advance, 0)

    for g in range(GROUPS):
        summed = total[g]
        result = (summed[:, :HEAD_DIM] / summed[:, HEAD_DIM:]).astype(jnp.bfloat16)
        result = jnp.concatenate(
            [result[j * TILE : (j + 1) * TILE] for j in range(PER_CORE)], axis=1
        )
        obuf[2 * g : 2 * g + 2] = result.reshape(2, NC, ROWS, QCOLS)
    mine = out_ref.at[:, columns(z * NC + core, QCOLS)]
    for d in order + (0,):
        for e in range(NC):
            to = ahead(z, d, NZ)
            to_core = (core + e) % NC
            source = obuf.at[to, to_core]
            if d == 0 and e == 0:
                pltpu.make_async_copy(source, mine, o_recv.at[0, 0]).start()
                continue
            sends.append(
                send(source, mine, o_send.at[d, e], o_recv.at[d, e], device(x, y, to, to_core))
            )
            sends[-1].start()
    for d in range(NZ):
        for e in range(NC):
            came = columns(back(z, d, NZ) * NC + (core + e) % NC, QCOLS)
            wait_in(out_ref.at[:, came], o_recv.at[d, e])
    for copy in sends:
        copy.wait_send()
    for dx in range(NX):
        at = back(x, dx, NX)
        to_sibling(kbuf, at, dx * 2).wait_send()
        to_sibling(vbuf, at, dx * 2 + 1).wait_send()


def body(queries, keys, values, tile_mask, noise_level, level_gate):
    dma = pltpu.SemaphoreType.DMA
    attended = pl.pallas_call(
        kernel,
        out_shape=jax.ShapeDtypeStruct(queries.shape, jnp.bfloat16),
        in_specs=[
            pl.BlockSpec(memory_space=pl.ANY),
            pl.BlockSpec(memory_space=pl.ANY),
            pl.BlockSpec(memory_space=pl.ANY),
            pl.BlockSpec(memory_space=pltpu.VMEM),
        ],
        out_specs=pl.BlockSpec(memory_space=pl.ANY),
        scratch_shapes=[
            pltpu.VMEM((NC, NX, NZ, NY, ROWS, HEAD_DIM), jnp.bfloat16),
            pltpu.VMEM((NC, NX, NZ, NY, ROWS, HEAD_DIM), jnp.bfloat16),
            pltpu.VMEM((NZ, NC, ROWS, QCOLS), jnp.bfloat16),
            pltpu.VMEM((NZ, NC, ROWS, QCOLS), jnp.bfloat16),
            pltpu.VMEM((GROUPS, TILE, HEAD_DIM), jnp.bfloat16),
            pltpu.VMEM((GROUPS, PER_CORE * TILE, HEAD_DIM), jnp.float32),
            pltpu.VMEM((GROUPS, PER_CORE * TILE, 2 * HEAD_DIM), jnp.float32),
            dma((NZ,)),
            dma((NZ,)),
            dma((NZ,)),
            dma((NZ,)),
            dma((NZ, NC)),
            dma((NZ, NC)),
            dma((NX,)),
            dma((NX,)),
            dma((NX, NY)),
            dma((NX, NY)),
            dma((NY,)),
            dma((NY,)),
            dma((NX, NY)),
            dma((NX, NY)),
            dma((2 * NX,)),
            dma((2 * NX,)),
            dma((NZ, NC)),
            dma((NZ, NC)),
        ],
        compiler_params=pltpu.CompilerParams(
            collective_id=0, has_side_effects=True, vmem_limit_bytes=48 * 1024 * 1024
        ),
    )(queries, keys, values, tile_mask)
    own_group = lax.axis_index("span") // (lax.axis_size("span") // GROUPS)
    gate_row = lax.dynamic_index_in_dim(
        level_gate, lax.dynamic_index_in_dim(noise_level, own_group, 0, False), 0
    )
    return (attended.astype(jnp.float32) * gate_row).astype(jnp.bfloat16)


def solution(mesh):
    return jax.shard_map(
        body,
        mesh=mesh,
        in_specs=(
            P(("span", "head"), None),
            P(("span", "head"), None),
            P(("span", "head"), None),
            P(),
            P(),
            P(),
        ),
        out_specs=P(("span", "head"), None),
        check_vma=False,
    )
```

time: 245 us -> 61.4 us (0.25)
  the two profiles are of different devices: /device:TPU:192 before, /device:TPU:1 now
where the time goes in v1:
time: 61.4 us; the launch traced here: 61.2 us
  Pallas kernels  55.3 us (90%)
  local copies, waits for them, and re-layouts  3.16 us (5%)
  between operations  2 us (3%)
  other arithmetic  0.81 us (1%)
    pallas_call x1, Pallas kernels, body(): pl.pallas_call(kernel, out_shape=jax.ShapeDtypeStruct(queries.shape, jnp....  55.3 us
    unnamed x10, local copies, waits for them, and re-layouts  1.84 us
    dynamic_slice x1, local copies, waits for them, and re-layouts, body(): lax.dynamic_index_in_dim(noise_level, own_group, 0, False)  1.29 us

profile of v1, /device:TPU:1, one launch (start us, length us, event | category | flops | bytes accessed | tf_op | source)
XLA Modules:
  0.0 61.2 jit_solution(3190874270305538593)
XLA Ops:
  0.0 0.0 copy-start
  0.0 0.0 copy-start.2
  0.0 0.0 copy-start.4
  0.0 1.3 %dynamic_slice.8 = s32[1]{0:T(128)} dynamic-slice(s32[4]{0:T(128)} %param.10, s32[]{:T(128)S(6)} %select_n.14), dynamic_slice_sizes={1} | dynamic-slice | bytes 12 | tf_op jit(solution)/shard_map/jit(dynamic_index_in_dim)/dynamic_slice | solution.py:356
  3.3 0.0 copy-done
  3.3 0.0 copy-done.2
  3.3 0.0 copy-done.4
  3.3 0.0 copy-start.1
  3.3 1.0 %copy-done.1 = bf16[32,6144]{1,0:T(8,128)(2,1)S(1)} copy-done((bf16[32,6144]{1,0:T(8,128)(2,1)S(1)}, bf16[32,6144]{1,0:T(8,128)(2,1)}, u32[]{:S(2)}) %copy-start.1) | copy-done | bytes 393240
  4.3 0.0 copy-start.3
  4.3 0.8 %copy-done.3 = bf16[32,1024]{1,0:T(8,128)(2,1)S(1)} copy-done((bf16[32,1024]{1,0:T(8,128)(2,1)S(1)}, bf16[32,1024]{1,0:T(8,128)(2,1)}, u32[]{:S(2)}) %copy-start.3) | copy-done | bytes 65560
  5.2 55.3 %shard_map.64 = bf16[32,6144]{1,0:T(8,128)(2,1)S(1)} custom-call(bf16[32,6144]{1,0:T(8,128)(2,1)S(1)} %copy-done.1, bf16[32,1024]{1,0:T(8,128)(2,1)S(1)} %copy-done.2, bf16[32,1024]{1,0:T(8,128)(2,1)S(1)} %copy-done.3, s32[4,16,64]{2,1,0:T(8,128)S(1)} %copy-done.4), custom_call_target="tpu_custom_call" | custom-call | tf_op jit(solution)/shard_map/pallas_call | solution.py:313
  60.4 0.8 %multiply_convert_fusion = bf16[32,6144]{1,0:T(8,128)(2,1)} fusion(bf16[32,6144]{1,0:T(8,128)(2,1)S(1)} %shard_map.64, f32[6144]{0:T(1024)S(1)} %bitcast.2), kind=kLoop, calls=%fused_computation | loop fusion | flops 589824 | bytes 811008 | tf_op jit(solution)/shard_map/convert_element_type | solution.py:358
  (1 shorter events, 0.0 us)
Async XLA Ops:
  0.0 3.3 %copy-start = (f32[16,6144]{1,0:T(8,128)S(1)}, f32[16,6144]{1,0:T(8,128)}, u32[]{:S(2)}) copy-start(f32[16,6144]{1,0:T(8,128)} %param.11) | copy-start | bytes 1179652
  0.0 3.3 %copy-start.2 = (bf16[32,1024]{1,0:T(8,128)(2,1)S(1)}, bf16[32,1024]{1,0:T(8,128)(2,1)}, u32[]{:S(2)}) copy-start(bf16[32,1024]{1,0:T(8,128)(2,1)} %k_hbm.1) | copy-start | bytes 196612
  0.0 3.3 %copy-start.4 = (s32[4,16,64]{2,1,0:T(8,128)S(1)}, s32[4,16,64]{2,1,0:T(8,128)}, u32[]{:S(2)}) copy-start(s32[4,16,64]{2,1,0:T(8,128)} %mask_ref.1) | copy-start | bytes 49156
  3.3 1.0 %copy-start.1 = (bf16[32,6144]{1,0:T(8,128)(2,1)S(1)}, bf16[32,6144]{1,0:T(8,128)(2,1)}, u32[]{:S(2)}) copy-start(bf16[32,6144]{1,0:T(8,128)(2,1)} %q_hbm.1) | copy-start | bytes 1179652
  4.3 0.8 %copy-start.3 = (bf16[32,1024]{1,0:T(8,128)(2,1)S(1)}, bf16[32,1024]{1,0:T(8,128)(2,1)}, u32[]{:S(2)}) copy-start(bf16[32,1024]{1,0:T(8,128)(2,1)} %v_hbm.1) | copy-start | bytes 196612

commit v2 on v0

v2 whole, which is shorter than its diff:
```python
import math

import jax
import jax.numpy as jnp
from jax import lax
from jax.experimental import pallas as pl
from jax.experimental.pallas import tpu as pltpu
from jax.sharding import PartitionSpec as P

HEADS = 48
KV_HEADS = 8
HEAD_DIM = 128
GROUPS = 4
TILE = 128
PER_KV = HEADS // KV_HEADS
PER_CORE = PER_KV // 2
ROWS = 32
QCOLS = PER_CORE * HEAD_DIM
SCALE = math.log2(math.e) / math.sqrt(HEAD_DIM)
BLOCKED = -1e30
MESH = pl.DeviceIdType.MESH
NX, NY, NZ, NC = 4, 4, 8, 2
GROUP_ROWS = PER_CORE * TILE
KEYS = 1024
VMEM_MIB = 58


def device(x, y, z, core):
    return (((z // 2) * NX + x) * NC + core, (z % 2) * NY + y)


def attend_step(c, far, core, kbuf, vbuf, query, top, total):
    keys = kbuf[far, c].reshape(KEYS, HEAD_DIM)
    values = vbuf[far, c].reshape(KEYS, HEAD_DIM)
    lane = lax.broadcasted_iota(jnp.int32, (TILE, HEAD_DIM), 1)
    source = (core + far) % NC
    marks = [
        (lane == (c * NX + kx) * 4 + source * 2 + low).astype(jnp.float32).astype(jnp.bfloat16)
        for kx in range(NX)
        for low in range(2)
    ]
    keys = jnp.concatenate([keys, jnp.concatenate(marks, axis=0)], axis=1)
    values = jnp.concatenate([values, jnp.ones_like(values)], axis=1)
    first = c * GROUP_ROWS
    scores = lax.dot_general(
        query[first:], keys, (((1,), (1,)), ((), ())), preferred_element_type=jnp.float32
    )
    old = top[first:]
    new = jnp.maximum(old, jnp.max(scores, axis=1, keepdims=True))
    factor = jnp.exp2((old - new) * SCALE)
    wide = jnp.concatenate([new] * (KEYS // HEAD_DIM), axis=1)
    weights = jnp.exp2((scores - wide) * SCALE).astype(jnp.bfloat16)
    part = lax.dot_general(
        weights, values, (((1,), (0,)), ((), ())), preferred_element_type=jnp.float32
    )
    total[first:] = total[first:] * jnp.concatenate([factor, factor], axis=1) + part
    top[first:] = new


def kernel(
    q_hbm,
    k_hbm,
    v_hbm,
    mask_hbm,
    level_hbm,
    gate_hbm,
    out_ref,
    gate_ref,
    kbuf,
    vbuf,
    qbuf,
    obuf,
    query,
    top,
    total,
    mask,
    gates,
    levels,
    side_sem,
    kz_send,
    kz_recv,
    vz_send,
    vz_recv,
    q_send,
    q_recv,
    kx_send,
    kx_recv,
    ky_send,
    ky_recv,
    vy_send,
    vy_recv,
    vx_send,
    vx_recv,
    sib_send,
    sib_recv,
    o_send,
    o_recv,
):
    span, head = lax.axis_index("span"), lax.axis_index("head")
    core = span % NC
    x = (span // NC) % NX
    z_hi, z_lo = span // (NC * NX), head // NY
    z = z_hi * 2 + z_lo
    y = head % NY

    def ahead(at, step, size):
        return (at + step) % size

    def back(at, step, size):
        return (at + size - step) % size

    sends = []

    def send(src, dst, send_sem, recv_sem, target):
        copy = pltpu.make_async_remote_copy(
            src_ref=src,
            dst_ref=dst,
            send_sem=send_sem,
            recv_sem=recv_sem,
            device_id=target,
            device_id_type=MESH,
        )
        copy.start()
        sends.append(copy)

    def wait_in(buf_at, sem):
        pltpu.make_async_copy(buf_at, buf_at, sem).wait()

    def columns(at, width):
        return pl.ds(pl.multiple_of(at * width, width), width)

    barrier = pltpu.get_barrier_semaphore()
    peers = [device(x, y, ahead(z, d, NZ), c) for d in range(1, NZ) for c in range(NC)]
    peers.append(device(x, y, z, 1 - core))
    peers += [device(ahead(x, d, NX), y, z, core) for d in range(1, NX)]
    peers += [device(x, ahead(y, d, NY), z, core) for d in range(1, NY)]
    for peer in peers:
        pl.semaphore_signal(barrier, inc=1, device_id=peer, device_id_type=MESH)
    sides = [
        pltpu.make_async_copy(mask_hbm, mask, side_sem.at[0]),
        pltpu.make_async_copy(level_hbm, levels, side_sem.at[1]),
        pltpu.make_async_copy(gate_hbm, gates, side_sem.at[2]),
    ]
    for copy in sides:
        copy.start()
    pl.semaphore_wait(barrier, len(peers))

    order = (4, 3, 5, 2, 6, 1, 7)
    for hbm, buf, send_sems, recv_sems in (
        (k_hbm, kbuf, kz_send, kz_recv),
        (v_hbm, vbuf, vz_send, vz_recv),
    ):
        place = buf.at[0, z_hi, x, z_lo, y]
        for d in order:
            to = ahead(z, d, NZ)
            send(
                hbm.at[:, columns(to, HEAD_DIM)],
                place,
                send_sems.at[d],
                recv_sems.at[z],
                device(x, y, to, core),
            )
        pltpu.make_async_copy(hbm.at[:, columns(z, HEAD_DIM)], place, recv_sems.at[z]).start()
    for d in order + (0,):
        for e in range(NC):
            to = ahead(z, d, NZ)
            to_core = (core + e) % NC
            source = q_hbm.at[:, columns(to * NC + to_core, QCOLS)]
            place = qbuf.at[z, core]
            if d == 0 and e == 0:
                pltpu.make_async_copy(source, place, q_recv.at[z, core]).start()
            else:
                send(
                    source, place, q_send.at[d, e], q_recv.at[z, core], device(x, y, to, to_core)
                )

    for c in range(GROUPS):
        for low in range(2):
            wait_in(kbuf.at[0, c, x, low, y], kz_recv.at[2 * c + low])
        chunk = kbuf.at[0, c, x, :, y]
        for d in (2, 1, 3):
            send(
                chunk, chunk, kx_send.at[c, d], kx_recv.at[c, d], device(ahead(x, d, NX), y, z, core)
            )
    for c in range(GROUPS):
        for low in range(2):
            wait_in(vbuf.at[0, c, x, low, y], vz_recv.at[2 * c + low])
        chunk = vbuf.at[0, c, x, :, y]
        for d in (2, 1, 3):
            send(
                chunk, chunk, vy_send.at[c, d], vy_recv.at[c, d], device(x, ahead(y, d, NY), z, core)
            )

    def prepare():
        top[...] = jnp.full_like(top, BLOCKED)
        total[...] = jnp.zeros_like(total)
        for copy in sides:
            copy.wait()
        gate_ref[...] = gates[pl.ds(levels[z_hi], 1), :]
        for g in range(GROUPS):
            for low in range(2):
                for c in range(NC):
                    row = mask[g, pl.ds((x * NC + c) * 2 + low, 1), :]
                    row = jnp.where(row > 0, 0.0, BLOCKED)
                    row = jnp.concatenate([row, jnp.zeros_like(row)], axis=1)
                    row = jnp.broadcast_to(row, (ROWS, HEAD_DIM)).astype(jnp.bfloat16)
                    for j in range(PER_CORE):
                        at = g * GROUP_ROWS + j * TILE + (low * NC + c) * ROWS
                        query[at : at + ROWS, HEAD_DIM:] = row

    rounds = {}

    def drain(c):
        for copy in rounds.pop(c):
            copy.wait_send()

    def spread(c):
        before = len(sends)
        for d in (1, 3, 2):
            wait_in(kbuf.at[0, c, back(x, d, NX), :, y], kx_recv.at[c, d])
        chunk = kbuf.at[0, c, :, :, y]
        for d in (2, 1, 3):
            send(
                chunk, chunk, ky_send.at[c, d], ky_recv.at[c, d], device(x, ahead(y, d, NY), z, core)
            )
        for d in (1, 3, 2):
            wait_in(vbuf.at[0, c, x, :, back(y, d, NY)], vy_recv.at[c, d])
        chunk = vbuf.at[0, c, x]
        for d in (2, 1, 3):
            send(
                chunk, chunk, vx_send.at[c, d], vx_recv.at[c, d], device(ahead(x, d, NX), y, z, core)
            )
        rounds[c] = sends[before:]
        del sends[before:]

    def take_queries():
        for at in range(NZ):
            for c in range(NC):
                wait_in(qbuf.at[at, c], q_recv.at[at, c])
        for g in range(GROUPS):
            rows = qbuf[2 * g : 2 * g + 2].reshape(TILE, QCOLS)
            for j in range(PER_CORE):
                at = g * GROUP_ROWS + j * TILE
                query[at : at + TILE, :HEAD_DIM] = rows[:, j * HEAD_DIM : (j + 1) * HEAD_DIM]

    def gathered(c):
        for d in range(1, NY):
            wait_in(kbuf.at[0, c, :, :, back(y, d, NY)], ky_recv.at[c, d])
        for d in range(1, NX):
            wait_in(vbuf.at[0, c, back(x, d, NX)], vx_recv.at[c, d])
        for n, buf in enumerate((kbuf, vbuf)):
            send(
                buf.at[0, c],
                buf.at[1, c],
                sib_send.at[c, n],
                sib_recv.at[c, n],
                device(x, y, z, 1 - core),
            )

    def finish(g):
        summed = total[g * GROUP_ROWS : (g + 1) * GROUP_ROWS]
        result = (summed[:, :HEAD_DIM] / summed[:, HEAD_DIM:]).astype(jnp.bfloat16)
        result = jnp.concatenate(
            [result[j * TILE : (j + 1) * TILE] for j in range(PER_CORE)], axis=1
        )
        obuf[2 * g : 2 * g + 2] = result.reshape(2, NC, ROWS, QCOLS)
        mine = out_ref.at[:, columns(z * NC + core, QCOLS)]
        for low in range(2):
            to = 2 * g + low
            for to_core in range(NC):
                source = obuf.at[to, to_core]
                own = jnp.logical_and(z == to, core == to_core)

                @pl.when(own)
                def _():
                    pltpu.make_async_copy(source, mine, o_recv.at[z, core]).start()

                @pl.when(jnp.logical_not(own))
                def _():
                    pltpu.make_async_remote_copy(
                        src_ref=source,
                        dst_ref=mine,
                        send_sem=o_send.at[to, to_core],
                        recv_sem=o_recv.at[z, core],
                        device_id=device(x, y, to, to_core),
                        device_id_type=MESH,
                    ).start()

    def attend(c, far):
        if far:
            for n, buf in enumerate((kbuf, vbuf)):
                wait_in(buf.at[1, c], sib_recv.at[c, n])
        attend_step(c, far, core, kbuf, vbuf, query, top, total)
        if far:
            finish(c)

    spread(0)
    prepare()
    drain(0)
    spread(1)
    take_queries()
    drain(1)
    spread(2)
    gathered(0)
    attend(0, 0)
    spread(3)
    gathered(1)
    attend(0, 1)
    attend(1, 0)
    gathered(2)
    attend(1, 1)
    attend(2, 0)
    gathered(3)
    attend(2, 1)
    attend(3, 0)
    attend(3, 1)

    for at in range(NZ):
        for c in range(NC):
            wait_in(out_ref.at[:, columns(at * NC + c, QCOLS)], o_recv.at[at, c])
    for copy in sum(rounds.values(), sends):
        copy.wait_send()
    for to in range(NZ):
        for to_core in range(NC):

            @pl.when(jnp.logical_not(jnp.logical_and(z == to, core == to_core)))
            def _():
                pltpu.make_async_copy(
                    obuf.at[to, to_core], obuf.at[to, to_core], o_send.at[to, to_core]
                ).wait()


def body(queries, keys, values, tile_mask, noise_level, level_gate):
    dma = pltpu.SemaphoreType.DMA
    buffer = pltpu.VMEM((NC, GROUPS, NX, 2, NY, ROWS, HEAD_DIM), jnp.bfloat16)
    pieces = pltpu.VMEM((NZ, NC, ROWS, QCOLS), jnp.bfloat16)
    hbm = pl.BlockSpec(memory_space=pltpu.HBM)
    attended, gate_row = pl.pallas_call(
        kernel,
        out_shape=(
            jax.ShapeDtypeStruct(queries.shape, jnp.bfloat16),
            jax.ShapeDtypeStruct((1, queries.shape[1]), jnp.float32),
        ),
        in_specs=[hbm] * 6,
        out_specs=(pl.BlockSpec(memory_space=pl.ANY), pl.BlockSpec(memory_space=pltpu.VMEM)),
        scratch_shapes=[
            buffer,
            buffer,
            pieces,
            pieces,
            pltpu.VMEM((GROUPS * GROUP_ROWS, 2 * HEAD_DIM), jnp.bfloat16),
            pltpu.VMEM((GROUPS * GROUP_ROWS, HEAD_DIM), jnp.float32),
            pltpu.VMEM((GROUPS * GROUP_ROWS, 2 * HEAD_DIM), jnp.float32),
            pltpu.VMEM(tile_mask.shape, jnp.int32),
            pltpu.VMEM(level_gate.shape, jnp.float32),
            pltpu.SMEM(noise_level.shape, jnp.int32),
            dma((3,)),
        ]
        + [dma((NZ,))] * 4
        + [dma((NZ, NC))] * 2
        + [dma((GROUPS, 4))] * 8
        + [dma((GROUPS, 2))] * 2
        + [dma((NZ, NC))] * 2,
        compiler_params=pltpu.CompilerParams(
            collective_id=0, has_side_effects=True, vmem_limit_bytes=VMEM_MIB * 1024 * 1024
        ),
    )(queries, keys, values, tile_mask, noise_level, level_gate)
    return (attended.astype(jnp.float32) * gate_row).astype(jnp.bfloat16)


def solution(mesh):
    return jax.shard_map(
        body,
        mesh=mesh,
        in_specs=(
            P(("span", "head"), None),
            P(("span", "head"), None),
            P(("span", "head"), None),
            P(),
            P(),
            P(),
        ),
        out_specs=P(("span", "head"), None),
        check_vma=False,
    )
```

time: 245 us -> 53.8 us (0.22)
  the two profiles are of different devices: /device:TPU:192 before, /device:TPU:1 now
where the time goes in v2:
time: 53.8 us; the launch traced here: 53.7 us
  Pallas kernels  51.9 us (96%)
  other arithmetic  1.81 us (3%)
    pallas_call x1, Pallas kernels, body(): pl.pallas_call(kernel, out_shape=(jax.ShapeDtypeStruct(queries.shape, jnp...  51.9 us
    convert_element_type x1, other arithmetic, body(): return (attended.astype(jnp.float32) * gate_row).astype(jnp.bfloat16)  1.81 us

profile of v2, /device:TPU:1, one launch (start us, length us, event | category | flops | bytes accessed | tf_op | source)
XLA Modules:
  0.0 53.7 jit_solution(11169145517077682)
XLA Ops:
  0.0 51.9 %shard_map.64 = (bf16[32,6144]{1,0:T(8,128)(2,1)}, f32[1,6144]{1,0:T(1,128)}) custom-call(bf16[32,6144]{1,0:T(8,128)(2,1)} %q_hbm.1, bf16[32,1024]{1,0:T(8,128)(2,1)} %k_hbm.1, bf16[32,1024]{1,0:T(8,128)(2,1)} %v_hbm.1, s32[4,16,64]{2,1,0:T(8,128)} %mask_hbm.1, s32[4]{0:T(128)} %level_hbm.1, f32[16,6144]{1,0:T(8,128)} %gate_hbm.1), custom_call_target="tpu_custom_call" | custom-call | tf_op jit(solution)/shard_map/pallas_call | solution.py:338
  51.9 1.8 %multiply_convert_fusion = bf16[32,6144]{1,0:T(8,128)(2,1)} fusion(bf16[32,6144]{1,0:T(8,128)(2,1)} %get-tuple-element.7, f32[6144]{0:T(1024)} %bitcast.1), kind=kLoop, calls=%fused_computation | loop fusion | flops 589824 | bytes 811008 | tf_op jit(solution)/shard_map/convert_element_type | solution.py:368

commit v3 on v2

v3 whole, which is shorter than its diff:
```python
import math

import jax
import jax.numpy as jnp
from jax import lax
from jax.experimental import pallas as pl
from jax.experimental.pallas import tpu as pltpu
from jax.sharding import PartitionSpec as P

HEADS = 48
KV_HEADS = 8
HEAD_DIM = 128
GROUPS = 4
TILE = 128
PER_KV = HEADS // KV_HEADS
ROWS = 32
QCOLS = PER_KV * HEAD_DIM
SCALE = math.log2(math.e) / math.sqrt(HEAD_DIM)
BLOCKED = -1e30
MESH = pl.DeviceIdType.MESH
NX, NY, NZ, NC = 4, 4, 8, 2
HALF = 2 * ROWS
PER_HALF = PER_KV // 2
HCOLS = PER_HALF * HEAD_DIM
GROUP_ROWS = PER_HALF * HALF
HALF_ROWS = GROUPS * GROUP_ROWS
KEYS = 1024
YIELD = (1, 2)
YIELD_FOR = (4, 5)
VMEM_MIB = 58


def device(x, y, z, core):
    return (((z // 2) * NX + x) * NC + core, (z % 2) * NY + y)


def attend_step(c, far, half, core, buf, query, top, total):
    keys = buf[far, c, 0].reshape(KEYS, HEAD_DIM)
    values = buf[far, c, 1].reshape(KEYS, HEAD_DIM)
    lane = lax.broadcasted_iota(jnp.int32, (TILE, HEAD_DIM), 1)
    source = (core + far) % NC
    marks = [
        (lane == (c * NX + kx) * 4 + source * 2 + low).astype(jnp.float32).astype(jnp.bfloat16)
        for kx in range(NX)
        for low in range(2)
    ]
    keys = jnp.concatenate([keys, jnp.concatenate(marks, axis=0)], axis=1)
    values = jnp.concatenate([values, jnp.ones_like(values)], axis=1)
    rows = slice(half * HALF_ROWS + c * GROUP_ROWS, (half + 1) * HALF_ROWS)
    scores = lax.dot_general(
        query[rows], keys, (((1,), (1,)), ((), ())), preferred_element_type=jnp.float32
    )
    old = top[rows]
    new = jnp.maximum(old, jnp.max(scores, axis=1, keepdims=True))
    factor = jnp.exp2((old - new) * SCALE)
    wide = jnp.concatenate([new] * (KEYS // HEAD_DIM), axis=1)
    weights = jnp.exp2((scores - wide) * SCALE).astype(jnp.bfloat16)
    part = lax.dot_general(
        weights, values, (((1,), (0,)), ((), ())), preferred_element_type=jnp.float32
    )
    total[rows] = total[rows] * jnp.concatenate([factor, factor], axis=1) + part
    top[rows] = new


def kernel(
    q_hbm,
    k_hbm,
    v_hbm,
    mask_hbm,
    level_hbm,
    gate_hbm,
    out_ref,
    gate_ref,
    buf,
    qbuf,
    obuf,
    query,
    top,
    total,
    mask,
    gates,
    levels,
    side_sem,
    kz_send,
    kz_recv,
    vz_send,
    vz_recv,
    q_send,
    q_recv,
    kx_send,
    kx_recv,
    ky_send,
    ky_recv,
    vy_send,
    vy_recv,
    vx_send,
    vx_recv,
    sib_send,
    sib_recv,
    o_send,
    o_recv,
):
    span, head = lax.axis_index("span"), lax.axis_index("head")
    core = span % NC
    x = (span // NC) % NX
    z_hi, z_lo = span // (NC * NX), head // NY
    z = z_hi * 2 + z_lo
    y = head % NY

    def ahead(at, step, size):
        return (at + step) % size

    def back(at, step, size):
        return (at + size - step) % size

    sends = []

    def send(src, dst, send_sem, recv_sem, target):
        copy = pltpu.make_async_remote_copy(
            src_ref=src,
            dst_ref=dst,
            send_sem=send_sem,
            recv_sem=recv_sem,
            device_id=target,
            device_id_type=MESH,
        )
        copy.start()
        sends.append(copy)

    def wait_in(buf_at, sem):
        pltpu.make_async_copy(buf_at, buf_at, sem).wait()

    def columns(at, width):
        return pl.ds(pl.multiple_of(at * width, width), width)

    barrier = pltpu.get_barrier_semaphore()
    peers = [device(x, y, ahead(z, d, NZ), core) for d in range(1, NZ)]
    peers.append(device(x, y, z, 1 - core))
    peers += [device(ahead(x, d, NX), y, z, core) for d in range(1, NX)]
    peers += [device(x, ahead(y, d, NY), z, core) for d in range(1, NY)]
    for peer in peers:
        pl.semaphore_signal(barrier, inc=1, device_id=peer, device_id_type=MESH)
    sides = [
        pltpu.make_async_copy(mask_hbm, mask, side_sem.at[0]),
        pltpu.make_async_copy(level_hbm, levels, side_sem.at[1]),
        pltpu.make_async_copy(gate_hbm, gates, side_sem.at[2]),
    ]
    for copy in sides:
        copy.start()
    pl.semaphore_wait(barrier, len(peers))

    order = (4, 3, 5, 2, 6, 1, 7)
    for n, hbm, send_sems, recv_sems in ((0, k_hbm, kz_send, kz_recv), (1, v_hbm, vz_send, vz_recv)):
        place = buf.at[0, z_hi, n, x, z_lo, y]
        for d in order:
            to = ahead(z, d, NZ)
            send(
                hbm.at[:, columns(to, HEAD_DIM)],
                place,
                send_sems.at[d],
                recv_sems.at[z],
                device(x, y, to, core),
            )
        pltpu.make_async_copy(hbm.at[:, columns(z, HEAD_DIM)], place, recv_sems.at[z]).start()
    def send_queries(half):
        place = qbuf.at[half, z]
        for d in order + (0,):
            to = ahead(z, d, NZ)
            source = q_hbm.at[:, columns(to * 2 + half, HCOLS)]
            if d:
                send(
                    source,
                    place,
                    q_send.at[half, d],
                    q_recv.at[half, z],
                    device(x, y, to, core),
                )
            else:
                pltpu.make_async_copy(source, place, q_recv.at[half, z]).start()

    def plane(c):
        for low in range(2):
            wait_in(buf.at[0, c, 0, x, low, y], kz_recv.at[2 * c + low])
        chunk = buf.at[0, c, 0, x, :, y]
        for d in (2, 1, 3):
            send(
                chunk, chunk, kx_send.at[c, d], kx_recv.at[c, d], device(ahead(x, d, NX), y, z, core)
            )
        for low in range(2):
            wait_in(buf.at[0, c, 1, x, low, y], vz_recv.at[2 * c + low])
        chunk = buf.at[0, c, 1, x, :, y]
        for d in (2, 1, 3):
            send(
                chunk, chunk, vy_send.at[c, d], vy_recv.at[c, d], device(x, ahead(y, d, NY), z, core)
            )

    def prepare():
        top[...] = jnp.full_like(top, BLOCKED)
        total[...] = jnp.zeros_like(total)
        for copy in sides:
            copy.wait()
        gate_ref[...] = gates[pl.ds(levels[z_hi], 1), :]
        for g in range(GROUPS):
            for low in range(2):
                row = mask[g, pl.ds((x * NC + core) * 2 + low, 1), :]
                row = jnp.where(row > 0, 0.0, BLOCKED)
                row = jnp.concatenate([row, jnp.zeros_like(row)], axis=1)
                row = jnp.broadcast_to(row, (ROWS, HEAD_DIM)).astype(jnp.bfloat16)
                for half in range(2):
                    for j in range(PER_HALF):
                        at = half * HALF_ROWS + g * GROUP_ROWS + j * HALF + low * ROWS
                        query[at : at + ROWS, HEAD_DIM:] = row

    def spread(c):
        for d in (1, 3, 2):
            wait_in(buf.at[0, c, 0, back(x, d, NX), :, y], kx_recv.at[c, d])
        chunk = buf.at[0, c, 0, :, :, y]
        for d in (2, 1, 3):
            send(
                chunk, chunk, ky_send.at[c, d], ky_recv.at[c, d], device(x, ahead(y, d, NY), z, core)
            )
        for d in (1, 3, 2):
            wait_in(buf.at[0, c, 1, x, :, back(y, d, NY)], vy_recv.at[c, d])
        chunk = buf.at[0, c, 1, x]
        for d in (2, 1, 3):
            send(
                chunk, chunk, vx_send.at[c, d], vx_recv.at[c, d], device(ahead(x, d, NX), y, z, core)
            )

    def take_queries(half):
        for at in range(NZ):
            wait_in(qbuf.at[half, at], q_recv.at[half, at])
        for g in range(GROUPS):
            rows = qbuf[half, 2 * g : 2 * g + 2].reshape(HALF, HCOLS)
            for j in range(PER_HALF):
                at = half * HALF_ROWS + g * GROUP_ROWS + j * HALF
                query[at : at + HALF, :HEAD_DIM] = rows[:, j * HEAD_DIM : (j + 1) * HEAD_DIM]

    def gathered(c):
        for d in range(1, NY):
            wait_in(buf.at[0, c, 0, :, :, back(y, d, NY)], ky_recv.at[c, d])
        for d in range(1, NX):
            wait_in(buf.at[0, c, 1, back(x, d, NX)], vx_recv.at[c, d])
        send(
            buf.at[0, c], buf.at[1, c], sib_send.at[c], sib_recv.at[c], device(x, y, z, 1 - core)
        )

    yields = jnp.logical_and(z >= YIELD[0], z <= YIELD[1])

    def finish(g):
        heads = []
        for half in range(2):
            at = half * HALF_ROWS + g * GROUP_ROWS
            summed = total[at : at + GROUP_ROWS]
            result = (summed[:, :HEAD_DIM] / summed[:, HEAD_DIM:]).astype(jnp.bfloat16)
            heads += [result[j * HALF : (j + 1) * HALF] for j in range(PER_HALF)]
        result = jnp.concatenate(heads, axis=1)
        obuf[2 * g : 2 * g + 2] = result.reshape(2, ROWS, QCOLS)
        mine = out_ref.at[:, columns(z, QCOLS)]
        if g == GROUPS - 1:

            @pl.when(yields)
            def _():
                for to in YIELD_FOR:
                    pltpu.make_async_copy(obuf.at[to], obuf.at[to], o_send.at[to]).wait()

        for to in (2 * g, 2 * g + 1):
            source = obuf.at[to]

            @pl.when(z == to)
            def _():
                pltpu.make_async_copy(source, mine, o_recv.at[z]).start()

            @pl.when(z != to)
            def _():
                pltpu.make_async_remote_copy(
                    src_ref=source,
                    dst_ref=mine,
                    send_sem=o_send.at[to],
                    recv_sem=o_recv.at[z],
                    device_id=device(x, y, to, core),
                    device_id_type=MESH,
                ).start()

    def attend(c, far, half):
        if far and half == 0:
            wait_in(buf.at[1, c], sib_recv.at[c])
        attend_step(c, far, half, core, buf, query, top, total)
        if far and half == 1:
            finish(c)

    send_queries(0)
    plane(0)
    plane(1)
    plane(2)
    plane(3)
    send_queries(1)
    spread(0)
    prepare()
    spread(1)
    take_queries(0)
    gathered(0)
    attend(0, 0, 0)
    spread(2)
    take_queries(1)
    attend(0, 0, 1)
    gathered(1)
    attend(0, 1, 0)
    attend(0, 1, 1)
    spread(3)
    attend(1, 0, 0)
    attend(1, 0, 1)
    gathered(2)
    attend(1, 1, 0)
    attend(1, 1, 1)
    attend(2, 0, 0)
    attend(2, 0, 1)
    gathered(3)
    attend(2, 1, 0)
    attend(2, 1, 1)
    attend(3, 0, 0)
    attend(3, 0, 1)
    attend(3, 1, 0)
    attend(3, 1, 1)

    for at in range(NZ):
        wait_in(out_ref.at[:, columns(at, QCOLS)], o_recv.at[at])
    for copy in sends:
        copy.wait_send()
    for to in range(NZ):
        left = z != to
        if to in YIELD_FOR:
            left = jnp.logical_and(left, jnp.logical_not(yields))

        @pl.when(left)
        def _():
            pltpu.make_async_copy(obuf.at[to], obuf.at[to], o_send.at[to]).wait()


def body(queries, keys, values, tile_mask, noise_level, level_gate):
    dma = pltpu.SemaphoreType.DMA
    buffer = pltpu.VMEM((NC, GROUPS, 2, NX, 2, NY, ROWS, HEAD_DIM), jnp.bfloat16)
    pieces = pltpu.VMEM((NZ, ROWS, QCOLS), jnp.bfloat16)
    hbm = pl.BlockSpec(memory_space=pltpu.HBM)
    attended, gate_row = pl.pallas_call(
        kernel,
        out_shape=(
            jax.ShapeDtypeStruct(queries.shape, jnp.bfloat16),
            jax.ShapeDtypeStruct((1, queries.shape[1]), jnp.float32),
        ),
        in_specs=[hbm] * 6,
        out_specs=(pl.BlockSpec(memory_space=pl.ANY), pl.BlockSpec(memory_space=pltpu.VMEM)),
        scratch_shapes=[
            buffer,
            pltpu.VMEM((2, NZ, ROWS, HCOLS), jnp.bfloat16),
            pieces,
            pltpu.VMEM((2 * HALF_ROWS, 2 * HEAD_DIM), jnp.bfloat16),
            pltpu.VMEM((2 * HALF_ROWS, HEAD_DIM), jnp.float32),
            pltpu.VMEM((2 * HALF_ROWS, 2 * HEAD_DIM), jnp.float32),
            pltpu.VMEM(tile_mask.shape, jnp.int32),
            pltpu.VMEM(level_gate.shape, jnp.float32),
            pltpu.SMEM(noise_level.shape, jnp.int32),
            dma((3,)),
        ]
        + [dma((NZ,))] * 4
        + [dma((2, NZ))] * 2
        + [dma((GROUPS, 4))] * 8
        + [dma((GROUPS,))] * 2
        + [dma((NZ,))] * 2,
        compiler_params=pltpu.CompilerParams(
            collective_id=0, has_side_effects=True, vmem_limit_bytes=VMEM_MIB * 1024 * 1024
        ),
    )(queries, keys, values, tile_mask, noise_level, level_gate)
    return (attended.astype(jnp.float32) * gate_row).astype(jnp.bfloat16)


def solution(mesh):
    return jax.shard_map(
        body,
        mesh=mesh,
        in_specs=(
            P(("span", "head"), None),
            P(("span", "head"), None),
            P(("span", "head"), None),
            P(),
            P(),
            P(),
        ),
        out_specs=P(("span", "head"), None),
        check_vma=False,
    )
```

time: 53.8 us -> 51.7 us (0.961)
  the two profiles are of different devices: /device:TPU:1 before, /device:TPU:192 now
where the time goes in v3:
time: 51.7 us; the launch traced here: 51.5 us
  Pallas kernels  49.7 us (96%)
  other arithmetic  1.81 us (4%)
    pallas_call x1, Pallas kernels, body(): pl.pallas_call(kernel, out_shape=(jax.ShapeDtypeStruct(queries.shape, jnp...  49.7 us
    convert_element_type x1, other arithmetic, body(): return (attended.astype(jnp.float32) * gate_row).astype(jnp.bfloat16)  1.81 us

profile of v3, /device:TPU:192, one launch (start us, length us, event | category | flops | bytes accessed | tf_op | source)
XLA Modules:
  0.0 51.5 jit_solution(17601427976348901654)
XLA Ops:
  0.0 49.7 %shard_map.64 = (bf16[32,6144]{1,0:T(8,128)(2,1)}, f32[1,6144]{1,0:T(1,128)}) custom-call(bf16[32,6144]{1,0:T(8,128)(2,1)} %q_hbm.1, bf16[32,1024]{1,0:T(8,128)(2,1)} %k_hbm.1, bf16[32,1024]{1,0:T(8,128)(2,1)} %v_hbm.1, s32[4,16,64]{2,1,0:T(8,128)} %mask_hbm.1, s32[4]{0:T(128)} %level_hbm.1, f32[16,6144]{1,0:T(8,128)} %gate_hbm.1), custom_call_target="tpu_custom_call" | custom-call | tf_op jit(solution)/shard_map/pallas_call | solution.py:345
  49.7 1.8 %multiply_convert_fusion = bf16[32,6144]{1,0:T(8,128)(2,1)} fusion(bf16[32,6144]{1,0:T(8,128)(2,1)} %get-tuple-element.7, f32[6144]{0:T(1024)} %bitcast.1), kind=kLoop, calls=%fused_computation | loop fusion | flops 589824 | bytes 811008 | tf_op jit(solution)/shard_map/convert_element_type | solution.py:374

commit v4 on v3

--- a/solution.py
+++ b/solution.py
@@ -70,7 +70,6 @@
     level_hbm,
     gate_hbm,
     out_ref,
-    gate_ref,
     buf,
     qbuf,
     obuf,
@@ -199,7 +198,6 @@
         total[...] = jnp.zeros_like(total)
         for copy in sides:
             copy.wait()
-        gate_ref[...] = gates[pl.ds(levels[z_hi], 1), :]
         for g in range(GROUPS):
             for low in range(2):
                 row = mask[g, pl.ds((x * NC + core) * 2 + low, 1), :]
@@ -254,7 +252,8 @@
             summed = total[at : at + GROUP_ROWS]
             result = (summed[:, :HEAD_DIM] / summed[:, HEAD_DIM:]).astype(jnp.bfloat16)
             heads += [result[j * HALF : (j + 1) * HALF] for j in range(PER_HALF)]
-        result = jnp.concatenate(heads, axis=1)
+        result = jnp.concatenate(heads, axis=1).astype(jnp.float32)
+        result = (result * gates[pl.ds(levels[g], 1), columns(z, QCOLS)]).astype(jnp.bfloat16)
         obuf[2 * g : 2 * g + 2] = result.reshape(2, ROWS, QCOLS)
         mine = out_ref.at[:, columns(z, QCOLS)]
         if g == GROUPS - 1:
@@ -342,14 +341,11 @@
     buffer = pltpu.VMEM((NC, GROUPS, 2, NX, 2, NY, ROWS, HEAD_DIM), jnp.bfloat16)
     pieces = pltpu.VMEM((NZ, ROWS, QCOLS), jnp.bfloat16)
     hbm = pl.BlockSpec(memory_space=pltpu.HBM)
-    attended, gate_row = pl.pallas_call(
+    return pl.pallas_call(
         kernel,
-        out_shape=(
-            jax.ShapeDtypeStruct(queries.shape, jnp.bfloat16),
-            jax.ShapeDtypeStruct((1, queries.shape[1]), jnp.float32),
-        ),
+        out_shape=pltpu.VMEM(queries.shape, jnp.bfloat16),
         in_specs=[hbm] * 6,
-        out_specs=(pl.BlockSpec(memory_space=pl.ANY), pl.BlockSpec(memory_space=pltpu.VMEM)),
+        out_specs=pl.BlockSpec(memory_space=pltpu.VMEM),
         scratch_shapes=[
             buffer,
             pltpu.VMEM((2, NZ, ROWS, HCOLS), jnp.bfloat16),
@@ -371,7 +367,6 @@
             collective_id=0, has_side_effects=True, vmem_limit_bytes=VMEM_MIB * 1024 * 1024
         ),
     )(queries, keys, values, tile_mask, noise_level, level_gate)
-    return (attended.astype(jnp.float32) * gate_row).astype(jnp.bfloat16)
 
 
 def solution(mesh):

time: 51.7 us -> 49.9 us (0.965)
  other arithmetic: 1.81 us -> 0 us
  local copies, waits for them, and re-layouts: 0 us -> 0.75 us
  Pallas kernels: 49.7 us -> 49 us
    convert_element_type x1 -> x0, other arithmetic: 1.81 us -> none  [body(): return (attended.astype(jnp.float32) * gate_row).astype(jnp.bfloat16)]
    unnamed x0 -> x1, local copies, waits for them, and re-layouts: none -> 0.75 us
    pallas_call x1, Pallas kernels: 49.7 us -> 49 us  [body(): pl.pallas_call(kernel, out_shape=pltpu.VMEM(queries.shape, jnp.bfloat16),...]
where the time goes in v4:
time: 49.9 us; the launch traced here: 49.8 us
  Pallas kernels  49 us (98%)
  local copies, waits for them, and re-layouts  0.75 us (2%)
    pallas_call x1, Pallas kernels, body(): pl.pallas_call(kernel, out_shape=pltpu.VMEM(queries.shape, jnp.bfloat16),...  49 us

profile of v4, /device:TPU:192, one launch (start us, length us, event | category | flops | bytes accessed | tf_op | source)
XLA Modules:
  0.0 49.8 jit_solution(14444661715016186009)
XLA Ops:
  0.0 49.0 %shard_map.64 = bf16[32,6144]{1,0:T(8,128)(2,1)S(1)} custom-call(bf16[32,6144]{1,0:T(8,128)(2,1)} %q_hbm.1, bf16[32,1024]{1,0:T(8,128)(2,1)} %k_hbm.1, bf16[32,1024]{1,0:T(8,128)(2,1)} %v_hbm.1, s32[4,16,64]{2,1,0:T(8,128)} %mask_hbm.1, s32[4]{0:T(128)} %level_hbm.1, f32[16,6144]{1,0:T(8,128)} %gate_hbm.1), custom_call_target="tpu_custom_call" | custom-call | tf_op jit(solution)/shard_map/pallas_call | solution.py:344
  49.0 0.7 %copy.8 = bf16[32,6144]{1,0:T(8,128)(2,1)} copy(bf16[32,6144]{1,0:T(8,128)(2,1)S(1)} %shard_map.64) | data formatting | bytes 786432

commit v5 on v4

--- a/solution.py
+++ b/solution.py
@@ -299,14 +299,14 @@
     spread(1)
     take_queries(0)
     gathered(0)
+    spread(2)
     attend(0, 0, 0)
-    spread(2)
     take_queries(1)
     attend(0, 0, 1)
+    spread(3)
     gathered(1)
     attend(0, 1, 0)
     attend(0, 1, 1)
-    spread(3)
     attend(1, 0, 0)
     attend(1, 0, 1)
     gathered(2)

time: 49.9 us -> 49.5 us (level)
  the two profiles are of different devices: /device:TPU:192 before, /device:TPU:8 now
where the time goes in v5:
time: 49.5 us; the launch traced here: 49.4 us
  Pallas kernels  48.6 us (98%)
  local copies, waits for them, and re-layouts  0.75 us (2%)
    pallas_call x1, Pallas kernels, body(): pl.pallas_call(kernel, out_shape=pltpu.VMEM(queries.shape, jnp.bfloat16),...  48.6 us

profile of v5, /device:TPU:8, one launch (start us, length us, event | category | flops | bytes accessed | tf_op | source)
XLA Modules:
  0.0 49.4 jit_solution(13778125315293977194)
XLA Ops:
  0.0 48.6 %shard_map.64 = bf16[32,6144]{1,0:T(8,128)(2,1)S(1)} custom-call(bf16[32,6144]{1,0:T(8,128)(2,1)} %q_hbm.1, bf16[32,1024]{1,0:T(8,128)(2,1)} %k_hbm.1, bf16[32,1024]{1,0:T(8,128)(2,1)} %v_hbm.1, s32[4,16,64]{2,1,0:T(8,128)} %mask_hbm.1, s32[4]{0:T(128)} %level_hbm.1, f32[16,6144]{1,0:T(8,128)} %gate_hbm.1), custom_call_target="tpu_custom_call" | custom-call | tf_op jit(solution)/shard_map/pallas_call | solution.py:344
  48.6 0.7 %copy.8 = bf16[32,6144]{1,0:T(8,128)(2,1)} copy(bf16[32,6144]{1,0:T(8,128)(2,1)S(1)} %shard_map.64) | data formatting | bytes 786432
